TPU v7x, 32 devices: a whole 2x2x4 slice. The times are simulated.
32 devices in a mesh: dp: 4 (over y, x), grid: 8 (over z, core).
Axes of the slice: x: 2, y: 2, z: 4, core: 2. Of those that a mesh axis runs over, the one named last changes fastest.
Arguments:
- intensities: bfloat16 [2048, 32, 128], P(('dp', 'grid')), may hold values from -6 to 6
- gridding: bfloat16 [2048, 32, 2048], P(('dp', 'grid')), may hold values from -0.0625 to 0.0625
- dest_slab: int32 [2048, 1], P(('dp', 'grid')), may hold values from 0 to 7; in each aligned block of 64 rows (0 to 63, 64 to 127, ...) at most 16 rows name the same one
- spectral_weights: float32 [4, 128, 128, 128], P('dp', None, 'grid'), may hold values from 0.05 to 2
Outputs:
- solution_field: float32 [128, 128, 128], P('grid')
- residual: float32 [128, 128, 128], P('grid')
Inputs may be any that keep to these rules, and one draw needn't show every extreme that they name: `dest_slab`: at most 16 of one device's 64 snapshots name the same slab, and in every draw some device has exactly 16 that name one slab.
All inputs are finite; a program needn't handle non-finite values.
Results may differ from a plain program's by a relative error of at most 0.0003.
Values may be sent and summed in bfloat16 or wider, within the bound.
A program may use at most 128 MiB of HBM per device.

v0:
```python
import math

import jax
import jax.numpy as jnp
from jax import lax
from jax.sharding import PartitionSpec as P

ITERS = 8


def tables(size):
    index = jnp.arange(size, dtype=jnp.int32)
    phase = index[:, None] * index[None, :] % size
    angle = phase.astype(jnp.float32) * (2.0 * math.pi / size)
    return (jnp.cos(angle), jnp.sin(angle))


def along(form, field, table):
    return jnp.einsum(form, field, table, precision=lax.Precision.HIGHEST)


def rotate(form, real_part, imag_part, cos_table, sin_table, sign):
    new_real = along(form, real_part, cos_table) - sign * along(form, imag_part, sin_table)
    new_imag = along(form, imag_part, cos_table) + sign * along(form, real_part, sin_table)
    return (new_real, new_imag)


def operate_slabs(field, weights, cos_table, sin_table):
    size = field.shape[1]
    first_real = along("ayz,zk->ayk", field, cos_table)
    first_imag = -along("ayz,zk->ayk", field, sin_table)
    mid_real, mid_imag = rotate("ayz,yk->akz", first_real, first_imag, cos_table, sin_table, -1.0)
    col_real, col_imag = (
        lax.all_to_all(mid_real, "grid", split_axis=1, concat_axis=0, tiled=True),
        lax.all_to_all(mid_imag, "grid", split_axis=1, concat_axis=0, tiled=True),
    )
    spec_real, spec_imag = rotate("ayz,ak->kyz", col_real, col_imag, cos_table, sin_table, -1.0)
    back_real, back_imag = rotate(
        "ayz,ak->kyz", weights * spec_real, weights * spec_imag, cos_table, sin_table, 1.0
    )
    plane_real, plane_imag = (
        lax.all_to_all(back_real, "grid", split_axis=0, concat_axis=1, tiled=True),
        lax.all_to_all(back_imag, "grid", split_axis=0, concat_axis=1, tiled=True),
    )
    row_real, row_imag = rotate("ayz,yk->akz", plane_real, plane_imag, cos_table, sin_table, 1.0)
    result = along("ayz,zk->ayk", row_real, cos_table) - along("ayz,zk->ayk", row_imag, sin_table)
    return result * (1.0 / (size * size * size))


def body(intensities, gridding, dest_slab, spectral_weights):
    ngrid = lax.axis_size("grid")
    ndp = lax.axis_size("dp")
    nent, rows, size = intensities.shape
    slab_rows = gridding.shape[2]
    planes = slab_rows // size
    capacity = max(2, 2 * nent // ngrid)
    target = dest_slab[:, 0]
    member = (target[:, None] == jnp.arange(ngrid, dtype=jnp.int32)[None, :]).astype(jnp.int32)
    before = jnp.sum((jnp.cumsum(member, axis=0) - member) * member, axis=1)
    slot = target * capacity + before
    value_slots = (
        jnp.zeros((ngrid * capacity, rows, size), intensities.dtype).at[slot].set(intensities)
    )
    matrix_slots = (
        jnp.zeros((ngrid * capacity, rows, slab_rows), gridding.dtype).at[slot].set(gridding)
    )
    value_dest = value_slots.reshape(ngrid, capacity * rows, size)
    matrix_dest = matrix_slots.reshape(ngrid, capacity * rows, slab_rows)
    product = lax.dot_general(
        matrix_dest, value_dest, (((1,), (1,)), ((0,), (0,))), preferred_element_type=jnp.float32
    )
    partial_value = lax.psum_scatter(
        product.reshape(slab_rows * lax.axis_size("grid"), size),
        "grid",
        scatter_dimension=0,
        tiled=True,
    )
    cos_table, sin_table = tables(size)
    quarter = size // ndp
    right_side = lax.psum(partial_value, "dp").reshape(planes, size, size)
    weights = lax.psum(spectral_weights[0], "dp")

    def operate(field):
        return operate_slabs(field, weights, cos_table, sin_table)

    def own_rows(field):
        return lax.dynamic_slice_in_dim(field, lax.axis_index("dp") * quarter, quarter, 1)

    def paired(residual, image):
        part = own_rows(residual)
        return lax.psum((jnp.sum(part * part), jnp.sum(part * own_rows(image))), ("dp", "grid"))

    solution_field = jnp.zeros_like(right_side)
    residual = right_side
    image = operate(residual)
    norm_now, product = paired(residual, image)
    alpha = norm_now / product
    direction, mapped = (residual, image)
    for step in range(ITERS):
        solution_field = solution_field + alpha * direction
        residual = residual - alpha * mapped
        if step + 1 < ITERS:
            image = operate(residual)
            norm_next, product = paired(residual, image)
            ratio = norm_next / norm_now
            alpha = norm_next / (product - ratio * norm_next / alpha)
            direction = residual + ratio * direction
            mapped = image + ratio * mapped
            norm_now = norm_next
    return (solution_field, residual)


def solution(mesh):
    return jax.shard_map(
        body,
        mesh=mesh,
        in_specs=(
            P(("dp", "grid"), None, None),
            P(("dp", "grid"), None, None),
            P(("dp", "grid"), None),
            P("dp", None, "grid", None),
        ),
        out_specs=(P("grid", None, None), P("grid", None, None)),
        check_vma=False,
    )
```

profile of v0, /device:TPU:0, one launch (start us, length us, event | category | flops | bytes accessed | tf_op | source)
XLA Modules:
  0.0 1838.6 jit_solution(4448234327897380169)
XLA Ops:
  9.5 6.1 broadcast_in_dim.4
  15.6 22.0 %scatter_fusion = bf16[128,32,2048]{2,1,0:T(8,128)(2,1)} fusion(bf16[128,32,2048]{2,1,0:T(8,128)(2,1)} %broadcast_in_dim.4, s32[64]{0:T(128)S(1)} %fusion.658, bf16[64,32,2048]{2,1,0:T(8,128)(2,1)} %param.5), kind=kCustom, calls=%fused_computation | custom fusion | bytes 25166080 | tf_op jit(solution)/shard_map/scatter | solution.py:65
  40.3 11.6 fusion.1139
  53.2 91.1 %reduce-scatter.2.cloned.1.call-done = f32[2048,128]{1,0:T(8,128)} async-done(((f32[16384,128]{1,0:T(8,128)}), f32[2048,128]{1,0:T(8,128)}) %reduce-scatter.2.cloned.1.call-update) | async-done | bytes 1048592 | tf_op jit(solution)/shard_map/reduce_scatter | solution.py:72
  144.4 71.9 %all-reduce.11.cloned.1.call-done = (f32[16,128,128]{2,1,0:T(8,128)}, f32[128,16,128]{2,0,1:T(8,128)}) async-done(((f32[16,128,128]{2,1,0:T(8,128)}, f32[128,16,128]{2,0,1:T(8,128)}), (f32[16,128,128]{2,1,0:T(8,128)}, f32[128,16,128]{2,0,1:T(8,128)})) %all-reduce.11.cloned.1.call-update) | async-done | bytes 2097168 | tf_op jit(solution)/shard_map/psum | solution.py:80
  225.4 4.9 all-to-all-start.1
  234.5 22.4 %all-to-all-done.1 = f32[16,128,128]{2,0,1:T(8,128)} async-done(((f32[16,128,128]{2,0,1:T(8,128)}), f32[16,128,128]{2,0,1:T(8,128)}, u32[]{:S(2)}, u32[]{:S(2)}) %all-to-all-start.1) | async-done | bytes 1048608 | tf_op jit(solution)/shard_map/all_to_all | solution.py:35
  264.1 22.9 %all-to-all-done = f32[16,128,128]{2,0,1:T(8,128)S(1)} async-done(((f32[16,128,128]{2,0,1:T(8,128)}), f32[16,128,128]{2,0,1:T(8,128)S(1)}, u32[]{:S(2)}, u32[]{:S(2)}) %all-to-all-start) | async-done | bytes 1048608 | tf_op jit(solution)/shard_map/all_to_all | solution.py:34
  299.9 4.7 all-to-all-start.3
  308.8 22.4 %all-to-all-done.3 = f32[128,16,128]{2,1,0:T(8,128)} async-done(((f32[128,16,128]{2,1,0:T(8,128)}), f32[128,16,128]{2,1,0:T(8,128)}, u32[]{:S(2)}, u32[]{:S(2)}) %all-to-all-start.3) | async-done | bytes 1048608 | tf_op jit(solution)/shard_map/all_to_all | solution.py:43
  338.4 22.9 %all-to-all-done.2 = f32[128,16,128]{2,1,0:T(8,128)S(1)} async-done(((f32[128,16,128]{2,1,0:T(8,128)}), f32[128,16,128]{2,1,0:T(8,128)S(1)}, u32[]{:S(2)}, u32[]{:S(2)}) %all-to-all-start.2) | async-done | bytes 1048608 | tf_op jit(solution)/shard_map/all_to_all | solution.py:42
  373.0 37.3 %all-reduce.7 = (f32[]{:T(128)}, f32[]{:T(128)}) all-reduce(f32[]{:T(128)} %get-tuple-element.17, f32[]{:T(128)} %get-tuple-element.16), channel_id=1, replica_groups=mesh['dp'=4,'grid'=8] {'dp','grid'}, use_global_device_ids=true, to_apply=%region_7.8 | all-reduce | flops 2 | bytes 16 | tf_op jit(solution)/shard_map/psum | solution.py:91
  430.5 20.1 %all-to-all-done.5 = f32[16,128,128]{2,0,1:T(8,128)} async-done(((f32[16,128,128]{2,0,1:T(8,128)}), f32[16,128,128]{2,0,1:T(8,128)}, u32[]{:S(2)}, u32[]{:S(2)}) %all-to-all-start.5) | async-done | bytes 1048608 | tf_op jit(solution)/shard_map/all_to_all | solution.py:35
  450.6 4.5 all-to-all-start.4
  459.7 22.0 %all-to-all-done.4 = f32[16,128,128]{2,0,1:T(8,128)} async-done(((f32[16,128,128]{2,0,1:T(8,128)}), f32[16,128,128]{2,0,1:T(8,128)}, u32[]{:S(2)}, u32[]{:S(2)}) %all-to-all-start.4) | async-done | bytes 1048608 | tf_op jit(solution)/shard_map/all_to_all | solution.py:34
  504.2 21.2 %all-to-all-done.7 = f32[128,16,128]{2,1,0:T(8,128)} async-done(((f32[128,16,128]{2,1,0:T(8,128)}), f32[128,16,128]{2,1,0:T(8,128)}, u32[]{:S(2)}, u32[]{:S(2)}) %all-to-all-start.7) | async-done | bytes 1048608 | tf_op jit(solution)/shard_map/all_to_all | solution.py:43
  525.4 4.6 all-to-all-start.6
  533.7 23.0 %all-to-all-done.6 = f32[128,16,128]{2,1,0:T(8,128)} async-done(((f32[128,16,128]{2,1,0:T(8,128)}), f32[128,16,128]{2,1,0:T(8,128)}, u32[]{:S(2)}, u32[]{:S(2)}) %all-to-all-start.6) | async-done | bytes 1048608 | tf_op jit(solution)/shard_map/all_to_all | solution.py:42
  566.5 39.3 %all-reduce.6 = (f32[]{:T(128)}, f32[]{:T(128)}) all-reduce(f32[]{:T(128)} %get-tuple-element.15, f32[]{:T(128)} %get-tuple-element.14), channel_id=1, replica_groups=mesh['dp'=4,'grid'=8] {'dp','grid'}, use_global_device_ids=true, to_apply=%region_12.13 | all-reduce | flops 2 | bytes 16 | tf_op jit(solution)/shard_map/psum | solution.py:91
  629.6 20.1 %all-to-all-done.9 = f32[16,128,128]{2,0,1:T(8,128)} async-done(((f32[16,128,128]{2,0,1:T(8,128)}), f32[16,128,128]{2,0,1:T(8,128)}, u32[]{:S(2)}, u32[]{:S(2)}) %all-to-all-start.9) | async-done | bytes 1048608 | tf_op jit(solution)/shard_map/all_to_all | solution.py:35
  649.7 4.5 all-to-all-start.8
  658.8 22.0 %all-to-all-done.8 = f32[16,128,128]{2,0,1:T(8,128)} async-done(((f32[16,128,128]{2,0,1:T(8,128)}), f32[16,128,128]{2,0,1:T(8,128)}, u32[]{:S(2)}, u32[]{:S(2)}) %all-to-all-start.8) | async-done | bytes 1048608 | tf_op jit(solution)/shard_map/all_to_all | solution.py:34
  705.5 20.0 %all-to-all-done.11 = f32[128,16,128]{2,1,0:T(8,128)} async-done(((f32[128,16,128]{2,1,0:T(8,128)}), f32[128,16,128]{2,1,0:T(8,128)}, u32[]{:S(2)}, u32[]{:S(2)}) %all-to-all-start.11) | async-done | bytes 1048608 | tf_op jit(solution)/shard_map/all_to_all | solution.py:43
  725.5 4.6 all-to-all-start.10
  734.8 22.0 %all-to-all-done.10 = f32[128,16,128]{2,1,0:T(8,128)} async-done(((f32[128,16,128]{2,1,0:T(8,128)}), f32[128,16,128]{2,1,0:T(8,128)}, u32[]{:S(2)}, u32[]{:S(2)}) %all-to-all-start.10) | async-done | bytes 1048608 | tf_op jit(solution)/shard_map/all_to_all | solution.py:42
  768.6 38.3 %all-reduce.5 = (f32[]{:T(128)}, f32[]{:T(128)}) all-reduce(f32[]{:T(128)} %get-tuple-element.13, f32[]{:T(128)} %get-tuple-element.12), channel_id=1, replica_groups=mesh['dp'=4,'grid'=8] {'dp','grid'}, use_global_device_ids=true, to_apply=%region_16.17 | all-reduce | flops 2 | bytes 16 | tf_op jit(solution)/shard_map/psum | solution.py:91
  820.5 4.2 all-to-all-start.13
  831.4 20.1 %all-to-all-done.13 = f32[16,128,128]{2,0,1:T(8,128)} async-done(((f32[16,128,128]{2,0,1:T(8,128)}), f32[16,128,128]{2,0,1:T(8,128)}, u32[]{:S(2)}, u32[]{:S(2)}) %all-to-all-start.13) | async-done | bytes 1048608 | tf_op jit(solution)/shard_map/all_to_all | solution.py:35
  851.4 4.4 all-to-all-start.12
  860.5 22.0 %all-to-all-done.12 = f32[16,128,128]{2,0,1:T(8,128)} async-done(((f32[16,128,128]{2,0,1:T(8,128)}), f32[16,128,128]{2,0,1:T(8,128)}, u32[]{:S(2)}, u32[]{:S(2)}) %all-to-all-start.12) | async-done | bytes 1048608 | tf_op jit(solution)/shard_map/all_to_all | solution.py:34
  896.4 4.2 all-to-all-start.15
  907.2 20.0 %all-to-all-done.15 = f32[128,16,128]{2,1,0:T(8,128)} async-done(((f32[128,16,128]{2,1,0:T(8,128)}), f32[128,16,128]{2,1,0:T(8,128)}, u32[]{:S(2)}, u32[]{:S(2)}) %all-to-all-start.15) | async-done | bytes 1048608 | tf_op jit(solution)/shard_map/all_to_all | solution.py:43
  927.2 4.6 all-to-all-start.14
  936.5 21.9 %all-to-all-done.14 = f32[128,16,128]{2,1,0:T(8,128)} async-done(((f32[128,16,128]{2,1,0:T(8,128)}), f32[128,16,128]{2,1,0:T(8,128)}, u32[]{:S(2)}, u32[]{:S(2)}) %all-to-all-start.14) | async-done | bytes 1048608 | tf_op jit(solution)/shard_map/all_to_all | solution.py:42
  971.2 39.2 %all-reduce.4 = (f32[]{:T(128)}, f32[]{:T(128)}) all-reduce(f32[]{:T(128)} %get-tuple-element.11, f32[]{:T(128)} %get-tuple-element.10), channel_id=1, replica_groups=mesh['dp'=4,'grid'=8] {'dp','grid'}, use_global_device_ids=true, to_apply=%region_20.21 | all-reduce | flops 2 | bytes 16 | tf_op jit(solution)/shard_map/psum | solution.py:91
  1033.8 20.0 %all-to-all-done.17 = f32[16,128,128]{2,0,1:T(8,128)} async-done(((f32[16,128,128]{2,0,1:T(8,128)}), f32[16,128,128]{2,0,1:T(8,128)}, u32[]{:S(2)}, u32[]{:S(2)}) %all-to-all-start.17) | async-done | bytes 1048608 | tf_op jit(solution)/shard_map/all_to_all | solution.py:35
  1053.9 4.4 all-to-all-start.16
  1062.9 22.0 %all-to-all-done.16 = f32[16,128,128]{2,0,1:T(8,128)} async-done(((f32[16,128,128]{2,0,1:T(8,128)}), f32[16,128,128]{2,0,1:T(8,128)}, u32[]{:S(2)}, u32[]{:S(2)}) %all-to-all-start.16) | async-done | bytes 1048608 | tf_op jit(solution)/shard_map/all_to_all | solution.py:34
  1109.8 19.9 %all-to-all-done.19 = f32[128,16,128]{2,1,0:T(8,128)} async-done(((f32[128,16,128]{2,1,0:T(8,128)}), f32[128,16,128]{2,1,0:T(8,128)}, u32[]{:S(2)}, u32[]{:S(2)}) %all-to-all-start.19) | async-done | bytes 1048608 | tf_op jit(solution)/shard_map/all_to_all | solution.py:43
  1129.7 4.6 all-to-all-start.18
  1138.9 22.0 %all-to-all-done.18 = f32[128,16,128]{2,1,0:T(8,128)} async-done(((f32[128,16,128]{2,1,0:T(8,128)}), f32[128,16,128]{2,1,0:T(8,128)}, u32[]{:S(2)}, u32[]{:S(2)}) %all-to-all-start.18) | async-done | bytes 1048608 | tf_op jit(solution)/shard_map/all_to_all | solution.py:42
  1173.7 38.3 %all-reduce.3 = (f32[]{:T(128)}, f32[]{:T(128)}) all-reduce(f32[]{:T(128)} %get-tuple-element.9, f32[]{:T(128)} %get-tuple-element.8), channel_id=1, replica_groups=mesh['dp'=4,'grid'=8] {'dp','grid'}, use_global_device_ids=true, to_apply=%region_24.25 | all-reduce | flops 2 | bytes 16 | tf_op jit(solution)/shard_map/psum | solution.py:91
  1236.9 20.0 %all-to-all-done.21 = f32[16,128,128]{2,0,1:T(8,128)} async-done(((f32[16,128,128]{2,0,1:T(8,128)}), f32[16,128,128]{2,0,1:T(8,128)}, u32[]{:S(2)}, u32[]{:S(2)}) %all-to-all-start.21) | async-done | bytes 1048608 | tf_op jit(solution)/shard_map/all_to_all | solution.py:35
  1256.9 4.4 all-to-all-start.20
  1266.0 22.0 %all-to-all-done.20 = f32[16,128,128]{2,0,1:T(8,128)} async-done(((f32[16,128,128]{2,0,1:T(8,128)}), f32[16,128,128]{2,0,1:T(8,128)}, u32[]{:S(2)}, u32[]{:S(2)}) %all-to-all-start.20) | async-done | bytes 1048608 | tf_op jit(solution)/shard_map/all_to_all | solution.py:34
  1312.8 19.9 %all-to-all-done.23 = f32[128,16,128]{2,1,0:T(8,128)} async-done(((f32[128,16,128]{2,1,0:T(8,128)}), f32[128,16,128]{2,1,0:T(8,128)}, u32[]{:S(2)}, u32[]{:S(2)}) %all-to-all-start.23) | async-done | bytes 1048608 | tf_op jit(solution)/shard_map/all_to_all | solution.py:43
  1332.8 4.6 all-to-all-start.22
  1342.0 22.0 %all-to-all-done.22 = f32[128,16,128]{2,1,0:T(8,128)} async-done(((f32[128,16,128]{2,1,0:T(8,128)}), f32[128,16,128]{2,1,0:T(8,128)}, u32[]{:S(2)}, u32[]{:S(2)}) %all-to-all-start.22) | async-done | bytes 1048608 | tf_op jit(solution)/shard_map/all_to_all | solution.py:42
  1376.9 39.2 %all-reduce.2 = (f32[]{:T(128)}, f32[]{:T(128)}) all-reduce(f32[]{:T(128)} %get-tuple-element.7, f32[]{:T(128)} %get-tuple-element.6), channel_id=1, replica_groups=mesh['dp'=4,'grid'=8] {'dp','grid'}, use_global_device_ids=true, to_apply=%region_28.29 | all-reduce | flops 2 | bytes 16 | tf_op jit(solution)/shard_map/psum | solution.py:91
  1439.3 20.1 %all-to-all-done.25 = f32[16,128,128]{2,0,1:T(8,128)} async-done(((f32[16,128,128]{2,0,1:T(8,128)}), f32[16,128,128]{2,0,1:T(8,128)}, u32[]{:S(2)}, u32[]{:S(2)}) %all-to-all-start.25) | async-done | bytes 1048608 | tf_op jit(solution)/shard_map/all_to_all | solution.py:35
  1459.3 4.5 all-to-all-start.24
  1468.4 22.0 %all-to-all-done.24 = f32[16,128,128]{2,0,1:T(8,128)} async-done(((f32[16,128,128]{2,0,1:T(8,128)}), f32[16,128,128]{2,0,1:T(8,128)}, u32[]{:S(2)}, u32[]{:S(2)}) %all-to-all-start.24) | async-done | bytes 1048608 | tf_op jit(solution)/shard_map/all_to_all | solution.py:34
  1515.2 20.0 %all-to-all-done.27 = f32[128,16,128]{2,1,0:T(8,128)} async-done(((f32[128,16,128]{2,1,0:T(8,128)}), f32[128,16,128]{2,1,0:T(8,128)}, u32[]{:S(2)}, u32[]{:S(2)}) %all-to-all-start.27) | async-done | bytes 1048608 | tf_op jit(solution)/shard_map/all_to_all | solution.py:43
  1535.2 4.7 all-to-all-start.26
  1544.5 22.0 %all-to-all-done.26 = f32[128,16,128]{2,1,0:T(8,128)} async-done(((f32[128,16,128]{2,1,0:T(8,128)}), f32[128,16,128]{2,1,0:T(8,128)}, u32[]{:S(2)}, u32[]{:S(2)}) %all-to-all-start.26) | async-done | bytes 1048608 | tf_op jit(solution)/shard_map/all_to_all | solution.py:42
  1579.2 38.3 %all-reduce.1 = (f32[]{:T(128)}, f32[]{:T(128)}) all-reduce(f32[]{:T(128)} %get-tuple-element.5, f32[]{:T(128)} %get-tuple-element.4), channel_id=1, replica_groups=mesh['dp'=4,'grid'=8] {'dp','grid'}, use_global_device_ids=true, to_apply=%region_32.33 | all-reduce | flops 2 | bytes 16 | tf_op jit(solution)/shard_map/psum | solution.py:91
  1642.6 20.1 %all-to-all-done.29 = f32[16,128,128]{2,0,1:T(8,128)} async-done(((f32[16,128,128]{2,0,1:T(8,128)}), f32[16,128,128]{2,0,1:T(8,128)}, u32[]{:S(2)}, u32[]{:S(2)}) %all-to-all-start.29) | async-done | bytes 1048608 | tf_op jit(solution)/shard_map/all_to_all | solution.py:35
  1662.7 4.5 all-to-all-start.28
  1671.7 22.0 %all-to-all-done.28 = f32[16,128,128]{2,0,1:T(8,128)} async-done(((f32[16,128,128]{2,0,1:T(8,128)}), f32[16,128,128]{2,0,1:T(8,128)}, u32[]{:S(2)}, u32[]{:S(2)}) %all-to-all-start.28) | async-done | bytes 1048608 | tf_op jit(solution)/shard_map/all_to_all | solution.py:34
  1716.6 20.0 %all-to-all-done.31 = f32[128,16,128]{2,1,0:T(8,128)} async-done(((f32[128,16,128]{2,1,0:T(8,128)}), f32[128,16,128]{2,1,0:T(8,128)}, u32[]{:S(2)}, u32[]{:S(2)}) %all-to-all-start.31) | async-done | bytes 1048608 | tf_op jit(solution)/shard_map/all_to_all | solution.py:43
  1736.6 4.5 all-to-all-start.30
  1745.8 22.0 %all-to-all-done.30 = f32[128,16,128]{2,1,0:T(8,128)} async-done(((f32[128,16,128]{2,1,0:T(8,128)}), f32[128,16,128]{2,1,0:T(8,128)}, u32[]{:S(2)}, u32[]{:S(2)}) %all-to-all-start.30) | async-done | bytes 1048608 | tf_op jit(solution)/shard_map/all_to_all | solution.py:42
  1780.6 39.1 %all-reduce = (f32[]{:T(128)}, f32[]{:T(128)}) all-reduce(f32[]{:T(128)} %get-tuple-element.3, f32[]{:T(128)} %get-tuple-element.2), channel_id=1, replica_groups=mesh['dp'=4,'grid'=8] {'dp','grid'}, use_global_device_ids=true, to_apply=%region_36.37 | all-reduce | flops 2 | bytes 16 | tf_op jit(solution)/shard_map/psum | solution.py:91
  1823.7 4.5 multiply_add_fusion
  (385 shorter events, 514.8 us)
Async XLA Ops:
  7.2 137.2 %reduce-scatter.2.cloned.1.call-start = ((), (), s32[]{:S(2)}) async-start(), calls=%async_computation.33 | async-start | bytes 9437184 | tf_op jit(solution)/shard_map/reduce_scatter | solution.py:72
  15.6 22.2 %copy-start.59 = (bf16[64,32,128]{2,1,0:T(8,128)(2,1)S(1)}, bf16[64,32,128]{2,1,0:T(8,128)(2,1)}, u32[]{:S(2)}) copy-start(bf16[64,32,128]{2,1,0:T(8,128)(2,1)} %param.4) | copy-start | bytes 1572868
  40.3 11.6 copy-start.58
  51.9 164.4 %all-reduce.11.cloned.1.call-start = ((), (), s32[]{:S(2)}) async-start(), calls=%async_computation.34 | async-start | bytes 4194304 | tf_op jit(solution)/shard_map/psum | solution.py:80
  216.2 74.4 %copy-start = (f32[128,16,128]{2,0,1:T(8,128)S(1)}, f32[128,16,128]{2,0,1:T(8,128)}, u32[]{:S(2)}) copy-start(f32[128,16,128]{2,0,1:T(8,128)} %get-tuple-element.35) | copy-start | bytes 3145732
  225.4 31.5 %all-to-all-start.1 = ((f32[16,128,128]{2,0,1:T(8,128)}), f32[16,128,128]{2,0,1:T(8,128)}, u32[]{:S(2)}, u32[]{:S(2)}) async-start(f32[16,128,128]{2,0,1:T(8,128)} %copy.436), calls=%async_computation.2 | async-start | bytes 2097152 | tf_op jit(solution)/shard_map/all_to_all | solution.py:35
  256.9 30.1 %all-to-all-start = ((f32[16,128,128]{2,0,1:T(8,128)}), f32[16,128,128]{2,0,1:T(8,128)S(1)}, u32[]{:S(2)}, u32[]{:S(2)}) async-start(f32[16,128,128]{2,0,1:T(8,128)} %copy.431), calls=%async_computation.1 | async-start | bytes 2097152 | tf_op jit(solution)/shard_map/all_to_all | solution.py:34
  261.8 28.8 %copy-start.44 = (f32[16,8,16,128]{3,0,1,2:T(8,128)}, f32[16,8,16,128]{3,0,1,2:T(8,128)S(1)}, u32[]{:S(2)}) copy-start(f32[16,8,16,128]{3,0,1,2:T(8,128)S(1)} %copy.437) | copy-start | bytes 3145732
  299.9 31.2 %all-to-all-start.3 = ((f32[128,16,128]{2,1,0:T(8,128)}), f32[128,16,128]{2,1,0:T(8,128)}, u32[]{:S(2)}, u32[]{:S(2)}) async-start(f32[128,16,128]{2,1,0:T(8,128)} %copy.448), calls=%async_computation.4 | async-start | bytes 2097152 | tf_op jit(solution)/shard_map/all_to_all | solution.py:43
  331.2 30.1 %all-to-all-start.2 = ((f32[128,16,128]{2,1,0:T(8,128)}), f32[128,16,128]{2,1,0:T(8,128)S(1)}, u32[]{:S(2)}, u32[]{:S(2)}) async-start(f32[128,16,128]{2,1,0:T(8,128)} %copy.443), calls=%async_computation.3 | async-start | bytes 2097152 | tf_op jit(solution)/shard_map/all_to_all | solution.py:42
  371.1 113.2 %copy-start.7 = (f32[16,128,128]{2,1,0:T(8,128)}, f32[16,128,128]{2,1,0:T(8,128)S(1)}, u32[]{:S(2)}) copy-start(f32[16,128,128]{2,1,0:T(8,128)S(1)} %convolution_subtract_fusion.21) | copy-start | bytes 3145732
  414.2 1.2 copy-start.11
  415.5 1.3 copy-start.24
  419.7 30.9 %all-to-all-start.5 = ((f32[16,128,128]{2,0,1:T(8,128)}), f32[16,128,128]{2,0,1:T(8,128)}, u32[]{:S(2)}, u32[]{:S(2)}) async-start(f32[16,128,128]{2,0,1:T(8,128)} %copy.460), calls=%async_computation.6 | async-start | bytes 2097152 | tf_op jit(solution)/shard_map/all_to_all | solution.py:35
  450.6 31.0 %all-to-all-start.4 = ((f32[16,128,128]{2,0,1:T(8,128)}), f32[16,128,128]{2,0,1:T(8,128)}, u32[]{:S(2)}, u32[]{:S(2)}) async-start(f32[16,128,128]{2,0,1:T(8,128)} %copy.455), calls=%async_computation.5 | async-start | bytes 2097152 | tf_op jit(solution)/shard_map/all_to_all | solution.py:34
  494.6 30.8 %all-to-all-start.7 = ((f32[128,16,128]{2,1,0:T(8,128)}), f32[128,16,128]{2,1,0:T(8,128)}, u32[]{:S(2)}, u32[]{:S(2)}) async-start(f32[128,16,128]{2,1,0:T(8,128)} %copy.472), calls=%async_computation.8 | async-start | bytes 2097152 | tf_op jit(solution)/shard_map/all_to_all | solution.py:43
  525.4 31.2 %all-to-all-start.6 = ((f32[128,16,128]{2,1,0:T(8,128)}), f32[128,16,128]{2,1,0:T(8,128)}, u32[]{:S(2)}, u32[]{:S(2)}) async-start(f32[128,16,128]{2,1,0:T(8,128)} %copy.467), calls=%async_computation.7 | async-start | bytes 2097152 | tf_op jit(solution)/shard_map/all_to_all | solution.py:42
  565.6 44.1 %copy-start.8 = (f32[16,128,128]{2,1,0:T(8,128)}, f32[16,128,128]{2,1,0:T(8,128)S(1)}, u32[]{:S(2)}) copy-start(f32[16,128,128]{2,1,0:T(8,128)S(1)} %fusion.54) | copy-start | bytes 3145732
  613.3 1.2 copy-start.12
  614.5 1.3 copy-start.25
  618.8 30.9 %all-to-all-start.9 = ((f32[16,128,128]{2,0,1:T(8,128)}), f32[16,128,128]{2,0,1:T(8,128)}, u32[]{:S(2)}, u32[]{:S(2)}) async-start(f32[16,128,128]{2,0,1:T(8,128)} %copy.484), calls=%async_computation.10 | async-start | bytes 2097152 | tf_op jit(solution)/shard_map/all_to_all | solution.py:35
  649.7 31.0 %all-to-all-start.8 = ((f32[16,128,128]{2,0,1:T(8,128)}), f32[16,128,128]{2,0,1:T(8,128)}, u32[]{:S(2)}, u32[]{:S(2)}) async-start(f32[16,128,128]{2,0,1:T(8,128)} %copy.479), calls=%async_computation.9 | async-start | bytes 2097152 | tf_op jit(solution)/shard_map/all_to_all | solution.py:34
  686.0 1.0 copy-start.33
  694.7 30.8 %all-to-all-start.11 = ((f32[128,16,128]{2,1,0:T(8,128)}), f32[128,16,128]{2,1,0:T(8,128)}, u32[]{:S(2)}, u32[]{:S(2)}) async-start(f32[128,16,128]{2,1,0:T(8,128)} %copy.496), calls=%async_computation.12 | async-start | bytes 2097152 | tf_op jit(solution)/shard_map/all_to_all | solution.py:43
  725.5 31.2 %all-to-all-start.10 = ((f32[128,16,128]{2,1,0:T(8,128)}), f32[128,16,128]{2,1,0:T(8,128)}, u32[]{:S(2)}, u32[]{:S(2)}) async-start(f32[128,16,128]{2,1,0:T(8,128)} %copy.491), calls=%async_computation.11 | async-start | bytes 2097152 | tf_op jit(solution)/shard_map/all_to_all | solution.py:42
  813.8 1.2 copy-start.1
  815.0 1.2 copy-start.14
  816.3 1.3 copy-start.26
  820.5 30.9 %all-to-all-start.13 = ((f32[16,128,128]{2,0,1:T(8,128)}), f32[16,128,128]{2,0,1:T(8,128)}, u32[]{:S(2)}, u32[]{:S(2)}) async-start(f32[16,128,128]{2,0,1:T(8,128)} %copy.508), calls=%async_computation.14 | async-start | bytes 2097152 | tf_op jit(solution)/shard_map/all_to_all | solution.py:35
  851.4 31.0 %all-to-all-start.12 = ((f32[16,128,128]{2,0,1:T(8,128)}), f32[16,128,128]{2,0,1:T(8,128)}, u32[]{:S(2)}, u32[]{:S(2)}) async-start(f32[16,128,128]{2,0,1:T(8,128)} %copy.503), calls=%async_computation.13 | async-start | bytes 2097152 | tf_op jit(solution)/shard_map/all_to_all | solution.py:34
  896.4 30.8 %all-to-all-start.15 = ((f32[128,16,128]{2,1,0:T(8,128)}), f32[128,16,128]{2,1,0:T(8,128)}, u32[]{:S(2)}, u32[]{:S(2)}) async-start(f32[128,16,128]{2,1,0:T(8,128)} %copy.520), calls=%async_computation.16 | async-start | bytes 2097152 | tf_op jit(solution)/shard_map/all_to_all | solution.py:43
  927.2 31.2 %all-to-all-start.14 = ((f32[128,16,128]{2,1,0:T(8,128)}), f32[128,16,128]{2,1,0:T(8,128)}, u32[]{:S(2)}, u32[]{:S(2)}) async-start(f32[128,16,128]{2,1,0:T(8,128)} %copy.515), calls=%async_computation.15 | async-start | bytes 2097152 | tf_op jit(solution)/shard_map/all_to_all | solution.py:42
  1016.2 1.2 copy-start.3
  1017.4 1.2 copy-start.16
  1018.7 1.3 copy-start.27
  1022.9 30.9 %all-to-all-start.17 = ((f32[16,128,128]{2,0,1:T(8,128)}), f32[16,128,128]{2,0,1:T(8,128)}, u32[]{:S(2)}, u32[]{:S(2)}) async-start(f32[16,128,128]{2,0,1:T(8,128)} %copy.532), calls=%async_computation.18 | async-start | bytes 2097152 | tf_op jit(solution)/shard_map/all_to_all | solution.py:35
  1053.9 31.0 %all-to-all-start.16 = ((f32[16,128,128]{2,0,1:T(8,128)}), f32[16,128,128]{2,0,1:T(8,128)}, u32[]{:S(2)}, u32[]{:S(2)}) async-start(f32[16,128,128]{2,0,1:T(8,128)} %copy.527), calls=%async_computation.17 | async-start | bytes 2097152 | tf_op jit(solution)/shard_map/all_to_all | solution.py:34
  1090.1 1.0 copy-start.35
  1098.9 30.8 %all-to-all-start.19 = ((f32[128,16,128]{2,1,0:T(8,128)}), f32[128,16,128]{2,1,0:T(8,128)}, u32[]{:S(2)}, u32[]{:S(2)}) async-start(f32[128,16,128]{2,1,0:T(8,128)} %copy.544), calls=%async_computation.20 | async-start | bytes 2097152 | tf_op jit(solution)/shard_map/all_to_all | solution.py:43
  1129.7 31.2 %all-to-all-start.18 = ((f32[128,16,128]{2,1,0:T(8,128)}), f32[128,16,128]{2,1,0:T(8,128)}, u32[]{:S(2)}, u32[]{:S(2)}) async-start(f32[128,16,128]{2,1,0:T(8,128)} %copy.539), calls=%async_computation.19 | async-start | bytes 2097152 | tf_op jit(solution)/shard_map/all_to_all | solution.py:42
  1219.3 1.2 copy-start.4
  1220.5 1.2 copy-start.18
  1221.8 1.3 copy-start.28
  1226.0 30.9 %all-to-all-start.21 = ((f32[16,128,128]{2,0,1:T(8,128)}), f32[16,128,128]{2,0,1:T(8,128)}, u32[]{:S(2)}, u32[]{:S(2)}) async-start(f32[16,128,128]{2,0,1:T(8,128)} %copy.556), calls=%async_computation.22 | async-start | bytes 2097152 | tf_op jit(solution)/shard_map/all_to_all | solution.py:35
  1256.9 31.0 %all-to-all-start.20 = ((f32[16,128,128]{2,0,1:T(8,128)}), f32[16,128,128]{2,0,1:T(8,128)}, u32[]{:S(2)}, u32[]{:S(2)}) async-start(f32[16,128,128]{2,0,1:T(8,128)} %copy.551), calls=%async_computation.21 | async-start | bytes 2097152 | tf_op jit(solution)/shard_map/all_to_all | solution.py:34
  1301.9 30.8 %all-to-all-start.23 = ((f32[128,16,128]{2,1,0:T(8,128)}), f32[128,16,128]{2,1,0:T(8,128)}, u32[]{:S(2)}, u32[]{:S(2)}) async-start(f32[128,16,128]{2,1,0:T(8,128)} %copy.568), calls=%async_computation.24 | async-start | bytes 2097152 | tf_op jit(solution)/shard_map/all_to_all | solution.py:43
  1332.8 31.2 %all-to-all-start.22 = ((f32[128,16,128]{2,1,0:T(8,128)}), f32[128,16,128]{2,1,0:T(8,128)}, u32[]{:S(2)}, u32[]{:S(2)}) async-start(f32[128,16,128]{2,1,0:T(8,128)} %copy.563), calls=%async_computation.23 | async-start | bytes 2097152 | tf_op jit(solution)/shard_map/all_to_all | solution.py:42
  1421.6 1.2 copy-start.5
  1422.9 1.2 copy-start.20
  1424.1 1.3 copy-start.29
  1428.4 30.9 %all-to-all-start.25 = ((f32[16,128,128]{2,0,1:T(8,128)}), f32[16,128,128]{2,0,1:T(8,128)}, u32[]{:S(2)}, u32[]{:S(2)}) async-start(f32[16,128,128]{2,0,1:T(8,128)} %copy.580), calls=%async_computation.26 | async-start | bytes 2097152 | tf_op jit(solution)/shard_map/all_to_all | solution.py:35
  1459.3 31.1 %all-to-all-start.24 = ((f32[16,128,128]{2,0,1:T(8,128)}), f32[16,128,128]{2,0,1:T(8,128)}, u32[]{:S(2)}, u32[]{:S(2)}) async-start(f32[16,128,128]{2,0,1:T(8,128)} %copy.575), calls=%async_computation.25 | async-start | bytes 2097152 | tf_op jit(solution)/shard_map/all_to_all | solution.py:34
  1504.4 30.8 %all-to-all-start.27 = ((f32[128,16,128]{2,1,0:T(8,128)}), f32[128,16,128]{2,1,0:T(8,128)}, u32[]{:S(2)}, u32[]{:S(2)}) async-start(f32[128,16,128]{2,1,0:T(8,128)} %copy.592), calls=%async_computation.28 | async-start | bytes 2097152 | tf_op jit(solution)/shard_map/all_to_all | solution.py:43
  1535.2 31.2 %all-to-all-start.26 = ((f32[128,16,128]{2,1,0:T(8,128)}), f32[128,16,128]{2,1,0:T(8,128)}, u32[]{:S(2)}, u32[]{:S(2)}) async-start(f32[128,16,128]{2,1,0:T(8,128)} %copy.587), calls=%async_computation.27 | async-start | bytes 2097152 | tf_op jit(solution)/shard_map/all_to_all | solution.py:42
  1624.9 1.2 copy-start.6
  1626.2 1.2 copy-start.22
  1627.4 1.3 copy-start.30
  1631.7 30.9 %all-to-all-start.29 = ((f32[16,128,128]{2,0,1:T(8,128)}), f32[16,128,128]{2,0,1:T(8,128)}, u32[]{:S(2)}, u32[]{:S(2)}) async-start(f32[16,128,128]{2,0,1:T(8,128)} %copy.604), calls=%async_computation.30 | async-start | bytes 2097152 | tf_op jit(solution)/shard_map/all_to_all | solution.py:35
  1662.7 31.1 %all-to-all-start.28 = ((f32[16,128,128]{2,0,1:T(8,128)}), f32[16,128,128]{2,0,1:T(8,128)}, u32[]{:S(2)}, u32[]{:S(2)}) async-start(f32[16,128,128]{2,0,1:T(8,128)} %copy.599), calls=%async_computation.29 | async-start | bytes 2097152 | tf_op jit(solution)/shard_map/all_to_all | solution.py:34
  1698.9 3.9 copy-start.31
  1702.8 1.3 copy-start.38
  1704.1 119.6 %copy-start.2 = (f32[16,128,128]{2,1,0:T(8,128)S(1)}, f32[16,128,128]{2,1,0:T(8,128)}, u32[]{:S(2)}) copy-start(f32[16,128,128]{2,1,0:T(8,128)} %copy-done.1) | copy-start | bytes 3145732
  1705.8 30.8 %all-to-all-start.31 = ((f32[128,16,128]{2,1,0:T(8,128)}), f32[128,16,128]{2,1,0:T(8,128)}, u32[]{:S(2)}, u32[]{:S(2)}) async-start(f32[128,16,128]{2,1,0:T(8,128)} %copy.616), calls=%async_computation.32 | async-start | bytes 2097152 | tf_op jit(solution)/shard_map/all_to_all | solution.py:43
  1736.6 31.1 %all-to-all-start.30 = ((f32[128,16,128]{2,1,0:T(8,128)}), f32[128,16,128]{2,1,0:T(8,128)}, u32[]{:S(2)}, u32[]{:S(2)}) async-start(f32[128,16,128]{2,1,0:T(8,128)} %copy.611), calls=%async_computation.31 | async-start | bytes 2097152 | tf_op jit(solution)/shard_map/all_to_all | solution.py:42
  (30 other events, 29.6 us)
Sparse Core Ops, SparseCore 0:
  52.0 92.3 reduce-scatter.1
  148.0 68.1 all-reduce.10
where the time goes:
time: 1850 us; the launch traced here: 1840 us
  waiting for transfers between devices  844 us (46%)
  blocking collectives  309 us (17%)
  matrix products  304 us (16%)
  local copies, waits for them, and re-layouts  158 us (9%)
  starting transfers between devices  140 us (8%)
  between operations  45.2 us (2%)
  other arithmetic  39.3 us (2%)
    psum x8, blocking collectives, paired(): lax.psum((jnp.sum(part * part), jnp.sum(part * own_rows(image))), ('dp',...  309 us
    dot_general x160, matrix products, along(): return jnp.einsum(form, field, table, precision=lax.Precision.HIGHEST)  293 us
    all_to_all x8, waiting for transfers between devices, operate_slabs(): lax.all_to_all(back_real, 'grid', split_axis=0, concat_axis=1, tiled=True)  178 us
    all_to_all x8, waiting for transfers between devices, operate_slabs(): lax.all_to_all(mid_real, 'grid', split_axis=1, concat_axis=0, tiled=True)  177 us
    all_to_all x8, waiting for transfers between devices, operate_slabs(): lax.all_to_all(back_imag, 'grid', split_axis=0, concat_axis=1, tiled=True)  163 us
    all_to_all x8, waiting for transfers between devices, operate_slabs(): lax.all_to_all(mid_imag, 'grid', split_axis=1, concat_axis=0, tiled=True)  163 us
    reduce_scatter x1, waiting for transfers between devices, body(): lax.psum_scatter(product.reshape(slab_rows * lax.axis_size('grid'), size)...  91.1 us
    psum x1, waiting for transfers between devices, body(): right_side = lax.psum(partial_value, 'dp').reshape(planes, size, size)  71.9 us
  transfers between devices with their start and end apart: 34, of which 34 were waited for; matrix products, arithmetic and copies ran while one was open for 9% of the time, Pallas kernels for 0%

commit v1 on v0

v1 whole, which is shorter than its diff:
```python
import functools
import math

import jax
import jax.numpy as jnp
import numpy as np
from jax import lax
from jax.experimental import pallas as pl
from jax.experimental.pallas import tpu as pltpu
from jax.sharding import PartitionSpec as P

ITERS = 8
HIGH = lax.Precision.HIGHEST


def half_size(size, ndp):
    return -(-(size // 2 + 1) // ndp)


def angles(rows, columns, size):
    return 2.0 * np.pi * ((rows[:, None] * columns[None, :]) % size) / size


def counts(size, kept):
    index = np.arange(kept)
    count = np.where((index == 0) | (2 * index == size), 1.0, 2.0)
    return np.where(2 * index > size, 0.0, count)


def first_table(size, ndp):
    each = half_size(size, ndp)
    index = np.arange(each * ndp)
    angle = angles(index, np.arange(size), size)
    table = np.stack([np.cos(angle), -np.sin(angle)])
    table = table * (counts(size, each * ndp) > 0)[None, :, None]
    return table.reshape(2, ndp, each, size).transpose(1, 0, 2, 3).astype(np.float32)


def last_table(size, ndp):
    each = half_size(size, ndp)
    index = np.arange(each * ndp)
    angle = angles(index, np.arange(size), size)
    table = np.stack([np.cos(angle), -np.sin(angle)])
    table = table * counts(size, each * ndp)[None, :, None] / float(size) ** 3
    return table.reshape(2, ndp, each, size).transpose(1, 0, 2, 3).astype(np.float32)


def complex_table(size, sign):
    angle = angles(np.arange(size), np.arange(size), size)
    cos, sin = np.cos(angle), sign * np.sin(angle)
    return np.stack([np.stack([cos, sin], 1), np.stack([-sin, cos], 1)]).astype(np.float32)


def along(form, field, table):
    return jnp.einsum(form, field, table, precision=HIGH)


def shared_sum(row, axis, count, inbox, outbox, send_sem, recv_sem, turn):
    me = lax.axis_index(axis)
    outbox[turn] = row
    copies = []
    for step in range(1, count):
        peer = lax.rem(me + step, count)
        copy = pltpu.make_async_remote_copy(
            src_ref=outbox.at[turn],
            dst_ref=inbox.at[turn, step - 1],
            send_sem=send_sem.at[turn, step - 1],
            recv_sem=recv_sem.at[turn, step - 1],
            device_id={axis: peer},
            device_id_type=pl.DeviceIdType.MESH,
        )
        copy.start()
        copies.append(copy)
    total = row
    for step in range(1, count):
        copies[step - 1].wait_recv()
        total = total + inbox[turn, step - 1]
    for copy in copies:
        copy.wait_send()
    return total


def scalar_kernel(ngrid, ndp, power_ref, weight_ref, rho_ref, sigma_ref,
                  delta_ref, grid_in, grid_out, dp_in, dp_out, gs, gr, ds, dr):
    me_grid, me_dp = lax.axis_index("grid"), lax.axis_index("dp")
    barrier = pltpu.get_barrier_semaphore()
    for step in range(1, ngrid):
        pl.semaphore_signal(barrier, inc=1, device_id={"grid": lax.rem(me_grid + step, ngrid)},
                            device_id_type=pl.DeviceIdType.MESH)
    for step in range(1, ndp):
        pl.semaphore_signal(barrier, inc=1, device_id={"dp": lax.rem(me_dp + step, ndp)},
                            device_id_type=pl.DeviceIdType.MESH)
    pl.semaphore_wait(barrier, ngrid + ndp - 2)
    lane = lax.broadcasted_iota(jnp.int32, (1, 128), 1)
    power, weight = power_ref[...], weight_ref[...]
    rho_ref[...] = jnp.ones_like(power)
    sigma_ref[...] = jnp.zeros_like(power)
    delta_ref[...] = jnp.zeros_like(power)

    def step(index, carry):
        norm_before, alpha_before = carry
        turn = lax.rem(index, 2)
        rho = rho_ref[...]
        square = rho * rho * power
        norm = jnp.sum(square)
        product = jnp.sum(square * weight)
        row = jnp.where(lane == 0, norm, jnp.where(lane == 1, product, 0.0))
        row = shared_sum(row, "grid", ngrid, grid_in, grid_out, gs, gr, turn)
        row = shared_sum(row, "dp", ndp, dp_in, dp_out, ds, dr, turn)
        norm = jnp.sum(jnp.where(lane == 0, row, 0.0), axis=1, keepdims=True)
        product = jnp.sum(jnp.where(lane == 1, row, 0.0), axis=1, keepdims=True)
        ratio = norm / norm_before
        first = jnp.full((1, 1), index, jnp.int32) == 0
        ratio = jnp.where(first, 0.0, ratio)
        product = product - jnp.where(first, 0.0, ratio * norm / alpha_before)
        alpha = norm / product
        delta = rho + ratio * delta_ref[...]
        delta_ref[...] = delta
        sigma_ref[...] = sigma_ref[...] + alpha * delta
        rho_ref[...] = rho - alpha * (weight * delta)
        return norm, alpha

    one = jnp.ones((1, 1), jnp.float32)
    lax.fori_loop(0, ITERS, step, (one, one))


def multipliers(power, weight):
    ngrid, ndp = lax.axis_size("grid"), lax.axis_size("dp")
    shape = jax.ShapeDtypeStruct(power.shape, jnp.float32)
    vmem = pl.BlockSpec(memory_space=pltpu.VMEM)
    dma = pltpu.SemaphoreType.DMA
    return pl.pallas_call(
        functools.partial(scalar_kernel, ngrid, ndp),
        out_shape=(shape, shape),
        in_specs=[vmem, vmem],
        out_specs=(vmem, vmem),
        scratch_shapes=[
            pltpu.VMEM(power.shape, jnp.float32),
            pltpu.VMEM((2, ngrid - 1, 1, 128), jnp.float32),
            pltpu.VMEM((2, 1, 128), jnp.float32),
            pltpu.VMEM((2, ndp - 1, 1, 128), jnp.float32),
            pltpu.VMEM((2, 1, 128), jnp.float32),
            dma((2, ngrid - 1)), dma((2, ngrid - 1)), dma((2, ndp - 1)), dma((2, ndp - 1)),
        ],
        compiler_params=pltpu.CompilerParams(collective_id=0, has_side_effects=True),
    )(power, weight)


def spectral_weight(weights, ngrid, ndp, each, size):
    turned = jnp.transpose(weights, (2, 1, 0))
    kept = each * ndp
    front = turned[:kept]
    back = jnp.roll(jnp.flip(turned, (0, 2)), (1, 1), (0, 2))[:kept]
    both = jnp.stack([front, back])
    both = both.reshape(2, ndp, each, both.shape[2], size).transpose(1, 0, 2, 3, 4)
    both = lax.psum_scatter(both, "dp", scatter_dimension=0, tiled=True)[0]
    front, back = both[0], both[1]
    edge = lax.ppermute(back[:, :1], "grid", [(g, (ngrid - g) % ngrid) for g in range(ngrid)])
    rest = lax.ppermute(back[:, 1:], "grid", [(g, ngrid - 1 - g) for g in range(ngrid)])
    back = jnp.concatenate([edge, jnp.flip(rest, 1)], axis=1)
    return 0.5 * (front + back)


def gridded(intensities, gridding, dest_slab, ngrid, ndp, each):
    nent, rows, size = intensities.shape
    slab_rows = gridding.shape[2]
    planes = slab_rows // size
    member = dest_slab == jnp.arange(ngrid, dtype=jnp.int32)[None, :]
    values = jnp.where(member[:, None, :, None], intensities[:, :, None, :], 0)
    values = values.reshape(nent * rows, ngrid * size)
    matrix = gridding.reshape(nent * rows, slab_rows)
    product = lax.dot_general(
        values, matrix, (((0,), (0,)), ((), ())), preferred_element_type=jnp.float32
    ).reshape(ngrid, size, slab_rows)
    table = first_table(size, ndp).reshape(ndp * 2 * each, size)
    spread = jnp.stack([
        lax.dot_general(jnp.asarray(table), product[s], (((1,), (0,)), ((), ())), precision=HIGH)
        for s in range(ngrid)
    ], axis=1).reshape(ndp, 2 * each, ngrid, slab_rows)
    part = lax.psum_scatter(spread, "dp", scatter_dimension=0, tiled=True)[0]
    part = jnp.transpose(part, (1, 0, 2))
    part = lax.psum_scatter(part, "grid", scatter_dimension=0, tiled=True)[0]
    return part.reshape(2, each, planes, size)


def body(intensities, gridding, dest_slab, spectral_weights):
    ngrid = lax.axis_size("grid")
    ndp = lax.axis_size("dp")
    nent, rows, size = intensities.shape
    each = half_size(size, ndp)
    weight = spectral_weight(spectral_weights[0], ngrid, ndp, each, size)
    part = gridded(intensities, gridding, dest_slab, ngrid, ndp, each)
    ahead, back = complex_table(size, -1.0), complex_table(size, 1.0)
    rows_done = along("ckxy,cydj->dkxj", part, ahead)
    columns = lax.all_to_all(rows_done, "grid", split_axis=3, concat_axis=2, tiled=True)
    spectrum = along("ckxj,cxdm->dkjm", columns, ahead)
    share = lax.dynamic_slice_in_dim(
        jnp.asarray(counts(size, each * ndp), jnp.float32), lax.axis_index("dp") * each, each
    )
    power = share[:, None, None] * (spectrum[0] * spectrum[0] + spectrum[1] * spectrum[1])
    rho, sigma = multipliers(power.reshape(-1, size), weight.reshape(-1, size))
    fields = jnp.stack([sigma, rho]).reshape((2, 1) + power.shape) * spectrum[None]
    columns = along("fckjm,cmdx->fdkxj", fields, back)
    planes = lax.all_to_all(columns, "grid", split_axis=3, concat_axis=4, tiled=True)
    planes = along("fckxj,cjdy->fdkxy", planes, back)
    whole = lax.all_gather(planes, "dp", axis=0, tiled=False)
    table = last_table(size, ndp)
    return tuple(along("dckxy,dckz->xyz", whole[:, f], table) for f in range(2))


def solution(mesh):
    return jax.shard_map(
        body,
        mesh=mesh,
        in_specs=(
            P(("dp", "grid"), None, None),
            P(("dp", "grid"), None, None),
            P(("dp", "grid"), None),
            P("dp", None, "grid", None),
        ),
        out_specs=(P("grid", None, None), P("grid", None, None)),
        check_vma=False,
    )
```

time: 1850 us -> 474 us (0.26)
  waiting for transfers between devices: 844 us -> 241 us
  blocking collectives: 309 us -> 18.6 us
  matrix products: 304 us -> 38.5 us
  starting transfers between devices: 140 us -> 7.06 us
  local copies, waits for them, and re-layouts: 158 us -> 80.2 us
  Pallas kernels: 0 us -> 60.8 us
  between operations: 45.2 us -> 14.7 us
  other arithmetic: 39.3 us -> 9.68 us
    all_to_all x32 -> x1, waiting for transfers between devices: 681 us -> 0.01 us  [body(): lax.all_to_all(rows_done, 'grid', split_axis=3, concat_axis=2, tiled=True)]
    psum x8 -> x0, blocking collectives: 309 us -> none  [paired(): lax.psum((jnp.sum(part * part), jnp.sum(part * own_rows(image))), ('dp',...]
    dot_general x161 -> x15, matrix products: 304 us -> 38.5 us  [the longest x8 15.4 us: gridded(): lax.dot_general(jnp.asarray(table), product[s], (((1,), (0,)), ((), ())),...]
    unnamed x2 -> x7, waiting for transfers between devices: 0.03 us -> 202 us
    all_to_all x32 -> x1, starting transfers between devices: 139 us -> 3.42 us  [body(): lax.all_to_all(rows_done, 'grid', split_axis=3, concat_axis=2, tiled=True)]
    reduce_scatter x1 -> x0, waiting for transfers between devices: 91.1 us -> none  [body(): lax.psum_scatter(product.reshape(slab_rows * lax.axis_size('grid'), size)...]
    psum x1 -> x0, waiting for transfers between devices: 71.9 us -> none  [body(): right_side = lax.psum(partial_value, 'dp').reshape(planes, size, size)]
    pallas_call x0 -> x1, Pallas kernels: none -> 60.8 us  [multipliers(): pl.pallas_call(functools.partial(scalar_kernel, ngrid, ndp), out_shape=(s...]
  transfers between devices with their start and end apart: 34 -> 7, of which waited for: 34 -> 5; matrix products, arithmetic and copies ran while one was open for 9% -> 3% of each run, Pallas kernels for 0% -> 0%
where the time goes in v1:
time: 474 us; the launch traced here: 470 us
  waiting for transfers between devices  241 us (51%)
  local copies, waits for them, and re-layouts  80.2 us (17%)
  Pallas kernels  60.8 us (13%)
  matrix products  38.5 us (8%)
  blocking collectives  18.6 us (4%)
  between operations  14.7 us (3%)
  other arithmetic  9.68 us (2%)
  starting transfers between devices  7.06 us (1%)
    unnamed x7, waiting for transfers between devices  202 us
    pallas_call x1, Pallas kernels, multipliers(): pl.pallas_call(functools.partial(scalar_kernel, ngrid, ndp), out_shape=(s...  60.8 us
    all_gather x1, waiting for transfers between devices, body(): whole = lax.all_gather(planes, 'dp', axis=0, tiled=False)  34.5 us
    unnamed x41, local copies, waits for them, and re-layouts  26.8 us
    another operation x10, local copies, waits for them, and re-layouts, gridded(): jnp.stack([lax.dot_general(jnp.asarray(table), product[s], (((1,), (0,)),...  25.2 us
    all_to_all x1, blocking collectives, body(): lax.all_to_all(columns, 'grid', split_axis=3, concat_axis=4, tiled=True)  18.6 us
    dot_general x8, matrix products, gridded(): lax.dot_general(jnp.asarray(table), product[s], (((1,), (0,)), ((), ())),...  15.4 us
    dot_general x1, matrix products, gridded(): lax.dot_general(values, matrix, (((0,), (0,)), ((), ())), preferred_eleme...  12.1 us
  transfers between devices with their start and end apart: 7, of which 5 were waited for; matrix products, arithmetic and copies ran while one was open for 3% of the time, Pallas kernels for 0%

profile of v1, /device:TPU:0, one launch (start us, length us, event | category | flops | bytes accessed | tf_op | source)
XLA Modules:
  0.0 470.0 jit_solution(652413465487539291)
XLA Ops:
  7.2 0.7 iota_compare_fusion
  7.9 1.6 broadcast_select_fusion
  9.6 12.1 %fusion = f32[1024,2048]{1,0:T(8,128)S(1)} fusion(bf16[2048,2048]{1,0:T(8,128)(2,1)} %bitcast.146, bf16[256,8,8,128]{3,2,1,0:T(8,128)(2,1)S(1)} %bitcast.137), kind=kOutput, calls=%fused_computation | convolution fusion | flops 8589934592 | bytes 20971520 | tf_op jit(solution)/shard_map/dot_general | solution.py:172
  21.7 1.0 fusion.7
  22.7 2.1 fusion.9
  24.8 2.0 fusion.11
  26.8 2.0 fusion.13
  28.9 2.0 fusion.15
  30.9 2.1 fusion.17
  33.0 2.1 fusion.19
  35.1 2.0 fusion.21
  37.2 1.4 stack.51
  38.6 2.5 stack.50
  41.1 2.5 stack.49
  43.5 2.4 stack.48
  46.0 2.4 stack.47
  48.4 2.5 stack.45
  50.9 2.4 stack.46
  53.4 1.6 constant_dynamic-update-slice_fusion.7
  55.6 0.9 copy-done.2
  57.0 0.9 copy-done
  58.3 8.8 %copy.56 = f32[4,34,8,2048]{3,2,1,0:T(8,128)} copy(f32[4,34,8,2048]{3,1,0,2:T(8,128)S(1)} %constant_dynamic-update-slice_fusion) | data formatting | bytes 17825792 | tf_op jit(solution)/shard_map/stack | solution.py:176
  67.2 93.5 %reduce-scatter.6.cloned.1.call-done = f32[1,34,8,2048]{3,2,1,0:T(8,128)} async-done(((f32[4,34,8,2048]{3,2,1,0:T(8,128)}), f32[1,34,8,2048]{3,2,1,0:T(8,128)}) %reduce-scatter.6.cloned.1.call-update) | async-done | bytes 2228240
  160.7 0.7 copy.62
  161.7 1.2 slice.102
  162.9 0.3 slice_maximum_fusion
  163.5 1.1 maximum_bitcast_fusion
  164.6 0.6 dynamic-slice.2
  165.2 0.6 dynamic-slice
  165.8 62.6 %all-reduce.6.cloned.1.call-done = f32[8,34,2048]{2,0,1:T(8,128)} async-done(((f32[8,34,2048]{2,0,1:T(8,128)}), f32[8,34,2048]{2,0,1:T(8,128)}) %all-reduce.6.cloned.1.call-update) | async-done | bytes 2228240
  228.4 2.5 constant_dynamic-slice_fusion.1
  230.9 0.4 convolution_bitcast_fusion.3
  231.3 1.9 copy.58
  233.2 2.5 reshape.128
  235.7 3.4 all-to-all-start
  239.2 45.8 %all-reduce.8.cloned.1.call-done = f32[4,2,17,16,128]{4,3,2,0,1:T(8,128)} async-done(((f32[4,2,17,16,128]{4,3,2,0,1:T(8,128)}), f32[4,2,17,16,128]{4,3,2,0,1:T(8,128)}) %all-reduce.8.cloned.1.call-update) | async-done | bytes 1114128
  285.0 1.6 constant_dynamic-slice_fusion
  286.7 2.8 collective-permute-start.1
  289.5 0.7 collective-permute-start
  290.4 4.1 collective-permute-done.1
  294.6 0.7 fusion.31.weight_ref
  295.3 0.5 broadcast.35
  295.8 1.3 reduce
  297.1 3.6 reshape.129
  300.7 3.8 copy.86
  304.6 0.6 reshape.107
  305.1 0.4 convolution_bitcast_fusion.2
  305.6 0.8 bitcast_multiply_fusion.power_ref
  306.3 60.8 %shard_map.131 = (f32[272,128]{1,0:T(8,128)}, f32[272,128]{1,0:T(8,128)}) custom-call(f32[272,128]{1,0:T(8,128)} %bitcast_multiply_fusion.power_ref, f32[272,128]{1,0:T(8,128)} %fusion.31.weight_ref), custom_call_target="tpu_custom_call" | custom-call | tf_op jit(solution)/shard_map/pallas_call | solution.py:132
  367.1 1.0 maximum_bitcast_fusion.1
  368.1 0.6 convolution_bitcast_fusion.1
  368.7 4.5 copy.63
  373.2 4.9 %reshape.130 = f32[8,1,17408]{2,1,0:T(1,128)S(1)} reshape(f32[128,2,2,16,17]{4,3,2,1,0:T(8,128)} %bitcast.130) | data formatting | bytes 1114112
  378.1 18.6 %all_to_all.36 = f32[8,1,17408]{2,1,0:T(1,128)S(1)} all-to-all(f32[8,1,17408]{2,1,0:T(1,128)S(1)} %reshape.130), channel_id=1, replica_groups=mesh['dp'=4,'grid'=8] {'grid'}, dimensions={0} | all-to-all | bytes 1114112 | tf_op jit(solution)/shard_map/all_to_all | solution.py:204
  396.7 1.9 reduce.1
  398.7 6.7 %reshape.131 = f32[128,2,2,16,17]{4,3,2,1,0:T(8,128)} reshape(f32[8,17408]{1,0:T(8,128)S(1)} %reduce.1) | data formatting | bytes 1114112
  405.4 7.2 %copy.89 = f32[2,2,17,16,8,16]{5,4,3,1,2,0:T(8,128)} copy(f32[2,2,17,16,8,16]{2,5,1,0,3,4:T(8,128)} %bitcast.131) | data formatting | bytes 1114112 | tf_op jit(solution)/shard_map/all_to_all | solution.py:204
  412.6 3.6 reshape.112
  416.3 0.6 convolution_bitcast_fusion
  416.9 0.8 copy.67
  417.8 34.5 %all-gather.3.cloned.1.call-done = f32[8,2,17,16,128]{4,3,2,1,0:T(8,128)} async-done(((f32[2,2,17,16,128]{4,3,2,1,0:T(8,128)}), f32[8,2,17,16,128]{4,3,2,1,0:T(8,128)}) %all-gather.3.cloned.1.call-update) | async-done | bytes 2228240 | tf_op jit(solution)/shard_map/all_gather | solution.py:206
  452.2 1.8 fusion.32
  454.0 4.5 fusion.6
  458.5 4.5 fusion.5
  (55 shorter events, 2.7 us)
Async XLA Ops:
  7.2 153.5 %reduce-scatter.6.cloned.1.call-start = ((), (), s32[]{:S(2)}) async-start(), calls=%async_computation.6 | async-start | bytes 11141120
  9.6 12.1 %copy-start.5 = (f32[136,128]{1,0:T(8,128)S(1)}, f32[136,128]{1,0:T(8,128)}, u32[]{:S(2)}) copy-start(f32[136,128]{1,0:T(8,128)} %constant.25.clone) | copy-start | bytes 208900
  53.4 1.7 copy-start.4
  53.4 2.1 copy-start.3
  55.1 1.4 copy-start.2
  55.5 1.4 copy-start.1
  56.5 1.4 copy-start
  67.1 93.6 %copy-start.7 = (f32[1,128,16,128]{3,2,1,0:T(8,128)S(1)}, f32[1,128,16,128]{3,2,1,0:T(8,128)}, u32[]{:S(2)}) copy-start(f32[1,128,16,128]{3,2,1,0:T(8,128)} %param.15) | copy-start | bytes 3145732
  67.1 161.3 %all-reduce.6.cloned.1.call-start = ((), (), s32[]{:S(2)}) async-start(), calls=%async_computation.4 | async-start | bytes 4456448
  160.7 124.3 %all-reduce.8.cloned.1.call-start = ((), (), s32[]{:S(2)}) async-start(), calls=%async_computation.5 | async-start | bytes 2228224
  163.4 1.2 copy-start.12
  163.5 1.7 copy-start.11
  163.5 67.4 %copy-start.6 = (f32[2,128,2,128,1]{3,1,0,2,4:T(8,128)S(1)}, f32[2,128,2,128,1]{3,1,0,2,4:T(8,128)}, u32[]{:S(2)}) copy-start(f32[2,128,2,128,1]{3,1,0,2,4:T(8,128)} %constant.43) | copy-start | bytes 786436
  233.2 57.0 %copy-start.10 = (f32[68]{0:T(128)S(1)}, f32[68]{0:T(128)}, u32[]{:S(2)}) copy-start(f32[68]{0:T(128)} %constant.27.clone) | copy-start | bytes 820
  235.7 59.6 %all-to-all-start = ((f32[8,1,8704]{2,1,0:T(1,128)}), f32[8,1,8704]{2,1,0:T(1,128)S(1)}, u32[]{:S(2)}, u32[]{:S(2)}) async-start(f32[8,1,8704]{2,1,0:T(1,128)} %reshape.128), calls=%async_computation | async-start | bytes 557056 | tf_op jit(solution)/shard_map/all_to_all | solution.py:195
  239.1 213.1 %all-gather.3.cloned.1.call-start = ((), (), s32[]{:S(2)}) async-start(), calls=%async_computation.3 | async-start | bytes 2785280 | tf_op jit(solution)/shard_map/all_gather | solution.py:206
  286.7 7.8 %collective-permute-start.1 = (f32[17,15,128]{2,1,0:T(8,128)S(1)}, f32[17,15,128]{2,1,0:T(8,128)S(1)}, u32[]{:S(2)}, u32[]{:S(2)}) collective-permute-start(f32[17,15,128]{2,1,0:T(8,128)S(1)} %slice.128), channel_id=1, source_target_pairs={{0,7},{1,6},{2,5},{3,4},{4,3},{5,2},{6,1},{7,0},{8,15},{9,14},{10,... | collective-permute-start | bytes 391688 | tf_op jit(solution)/shard_map/ppermute | solution.py:159
  289.5 5.1 %collective-permute-start = (f32[17,1,128]{2,1,0:T(1,128)S(1)}, f32[17,1,128]{2,1,0:T(1,128)S(1)}, u32[]{:S(2)}, u32[]{:S(2)}) collective-permute-start(f32[17,1,128]{2,1,0:T(1,128)S(1)} %slice.127), channel_id=1, source_target_pairs={{0,0},{1,7},{2,6},{3,5},{4,4},{5,3},{6,2},{7,1},{8,8},{9,15},{10,1... | collective-permute-start | bytes 26120 | tf_op jit(solution)/shard_map/ppermute | solution.py:158
  304.5 63.6 %copy-start.8 = (f32[2,128,2,128,1,1]{3,1,0,2,5,4:T(8,128)S(1)}, f32[2,128,2,128,1,1]{3,1,0,2,5,4:T(8,128)}, u32[]{:S(2)}) copy-start(f32[2,128,2,128,1,1]{3,1,0,2,5,4:T(8,128)} %constant.44) | copy-start | bytes 786436
  452.2 1.8 copy-start.9
Sparse Core Ops, SparseCore 0:
  67.2 93.3 reduce-scatter.5
  163.0 65.2 all-reduce.5
  231.8 53.2 all-reduce.7
  417.9 34.3 all-gather.2

commit v2 on v1

--- a/solution.py
+++ b/solution.py
@@ -13,36 +13,38 @@
 HIGH = lax.Precision.HIGHEST
 
 
-def half_size(size, ndp):
-    return -(-(size // 2 + 1) // ndp)
-
-
 def angles(rows, columns, size):
     return 2.0 * np.pi * ((rows[:, None] * columns[None, :]) % size) / size
 
 
-def counts(size, kept):
-    index = np.arange(kept)
-    count = np.where((index == 0) | (2 * index == size), 1.0, 2.0)
-    return np.where(2 * index > size, 0.0, count)
+def slot_index(size, ndp):
+    each = size // 2 // ndp
+    index = np.full((ndp, each + 1), size // 2)
+    index[:, :each] = np.arange(size // 2).reshape(ndp, each)
+    return index
+
+
+def counts(size, ndp):
+    index = slot_index(size, ndp)
+    count = np.where(index == 0, 1.0, 2.0)
+    count[:, -1] = 0.0
+    count[0, -1] = 1.0
+    return count.astype(np.float32)
 
 
 def first_table(size, ndp):
-    each = half_size(size, ndp)
-    index = np.arange(each * ndp)
-    angle = angles(index, np.arange(size), size)
-    table = np.stack([np.cos(angle), -np.sin(angle)])
-    table = table * (counts(size, each * ndp) > 0)[None, :, None]
-    return table.reshape(2, ndp, each, size).transpose(1, 0, 2, 3).astype(np.float32)
+    angle = angles(np.arange(size // 2), np.arange(size), size)
+    real, imag = np.cos(angle), -np.sin(angle)
+    imag[0] = np.cos(np.pi * np.arange(size))
+    table = np.stack([real, imag]).reshape(2, ndp, -1, size)
+    return table.transpose(1, 0, 2, 3).reshape(size, size).astype(np.float32)
 
 
 def last_table(size, ndp):
-    each = half_size(size, ndp)
-    index = np.arange(each * ndp)
-    angle = angles(index, np.arange(size), size)
-    table = np.stack([np.cos(angle), -np.sin(angle)])
-    table = table * counts(size, each * ndp)[None, :, None] / float(size) ** 3
-    return table.reshape(2, ndp, each, size).transpose(1, 0, 2, 3).astype(np.float32)
+    index = slot_index(size, ndp)
+    angle = angles(index.reshape(-1), np.arange(size), size).reshape(index.shape + (size,))
+    table = np.stack([np.cos(angle), -np.sin(angle)], 1)
+    return (table * counts(size, ndp)[:, None, :, None] / float(size) ** 3).astype(np.float32)
 
 
 def complex_table(size, sign):
@@ -146,14 +148,169 @@
     )(power, weight)
 
 
-def spectral_weight(weights, ngrid, ndp, each, size):
+def grid_kernel(ngrid, ndp, size, values_ref, matrix_ref, table_ref, weight_ref,
+                part_ref, total_ref, own, sibling, pair_in, dp_in, ready, group_in, weight_in,
+                pair_s, pair_r, dp_s, dp_r, group_s, group_r, weight_s, weight_r):
+    grid, dp = lax.axis_index("grid"), lax.axis_index("dp")
+    groups = ngrid // 2
+    core = lax.rem(grid, 2)
+    group = grid // 2
+    other = 2 * group + 1 - core
+    mesh_id = pl.DeviceIdType.MESH
+    barrier = pltpu.get_barrier_semaphore()
+    pl.semaphore_signal(barrier, inc=1, device_id={"grid": other}, device_id_type=mesh_id)
+    for step in range(1, groups):
+        peer = 2 * lax.rem(group + step, groups) + core
+        pl.semaphore_signal(barrier, inc=1, device_id={"grid": peer}, device_id_type=mesh_id)
+    for step in range(1, ndp):
+        pl.semaphore_signal(barrier, inc=1, device_id={"dp": lax.rem(dp + step, ndp)},
+                            device_id_type=mesh_id)
+    pl.semaphore_wait(barrier, groups + ndp - 1)
+
+    weight_copies = []
+    for step in range(1, ndp):
+        peer = lax.rem(dp + step, ndp)
+        copy = pltpu.make_async_remote_copy(
+            src_ref=weight_ref.at[peer], dst_ref=weight_in.at[step - 1],
+            send_sem=weight_s.at[step - 1], recv_sem=weight_r.at[step - 1],
+            device_id={"dp": peer}, device_id_type=mesh_id)
+        copy.start()
+        weight_copies.append(copy)
+
+    columns = matrix_ref.shape[1]
+    tile = math.gcd(columns, 512)
+    rows = size // ndp
+
+    def compute(step):
+        chunk = lax.rem(group + 1 + step, groups)
+
+        @pl.loop(0, columns // tile)
+        def _(index):
+            at = pl.ds(pl.multiple_of(index * tile, tile), tile)
+            product = jnp.dot(values_ref[chunk], matrix_ref[:, at],
+                              preferred_element_type=jnp.float32)
+            for half, buffer in enumerate((own, sibling)):
+                turned = jnp.dot(table_ref[...], product[half * size:(half + 1) * size],
+                                 precision=HIGH, preferred_element_type=jnp.float32)
+                buffer[step, :, :, at] = turned.reshape(ndp, rows, tile)
+
+    def send_pair(step):
+        copy = pltpu.make_async_remote_copy(
+            src_ref=sibling.at[step], dst_ref=pair_in.at[step],
+            send_sem=pair_s.at[step], recv_sem=pair_r.at[step],
+            device_id={"grid": other}, device_id_type=mesh_id)
+        copy.start()
+        return [copy]
+
+    def send_dp(step):
+        copies = []
+        for turn in range(1, ndp):
+            peer = lax.rem(dp + turn, ndp)
+            own[step, peer] = own[step, peer] + pair_in[step, peer]
+            copy = pltpu.make_async_remote_copy(
+                src_ref=own.at[step, peer], dst_ref=dp_in.at[step, turn - 1],
+                send_sem=dp_s.at[step, turn - 1], recv_sem=dp_r.at[step, turn - 1],
+                device_id={"dp": peer}, device_id_type=mesh_id)
+            copy.start()
+            copies.append(copy)
+        ready[step] = own[step, dp] + pair_in[step, dp]
+        return copies
+
+    def send_group(step):
+        total = ready[step]
+        for turn in range(ndp - 1):
+            total = total + dp_in[step, turn]
+        ready[step] = total
+        if step == groups - 1:
+            return []
+        peer = 2 * lax.rem(group + 1 + step, groups) + core
+        copy = pltpu.make_async_remote_copy(
+            src_ref=ready.at[step], dst_ref=group_in.at[step],
+            send_sem=group_s.at[step], recv_sem=group_r.at[step],
+            device_id={"grid": peer}, device_id_type=mesh_id)
+        copy.start()
+        return [copy]
+
+    pair_copies, dp_copies, group_copies = [], [], []
+    for step in range(groups + 2):
+        if step < groups:
+            compute(step)
+            pair_copies.append(send_pair(step))
+        if 1 <= step <= groups:
+            for copy in pair_copies[step - 1]:
+                copy.wait_recv()
+            dp_copies.append(send_dp(step - 1))
+        if step >= 2:
+            for copy in dp_copies[step - 2]:
+                copy.wait_recv()
+            group_copies.append(send_group(step - 2))
+    for copy in weight_copies:
+        copy.wait_recv()
+    total = weight_ref[dp]
+    for step in range(ndp - 1):
+        total = total + weight_in[step]
+    total_ref[...] = total
+    part = ready[groups - 1]
+    for step in range(groups - 1):
+        for copy in group_copies[step]:
+            copy.wait_recv()
+        part = part + group_in[step]
+    part_ref[...] = part
+    for copies in pair_copies + dp_copies + group_copies + [weight_copies]:
+        for copy in copies:
+            copy.wait_send()
+
+
+def gridded(intensities, gridding, dest_slab, weights, ngrid, ndp):
+    nent, rows, size = intensities.shape
+    slab_rows = gridding.shape[2]
+    core = lax.axis_index("grid") % 2
+    groups, share = ngrid // 2, size // ndp
+    slabs = 2 * np.arange(groups)[:, None] + jnp.stack([core, 1 - core])[None, :]
+    target = jnp.repeat(dest_slab[:, 0], rows)
+    member = target[None, None, :] == slabs[:, :, None]
+    turned = intensities.reshape(nent * rows, size).T
+    values = jnp.where(member[:, :, None, :], turned[None, None], 0)
+    values = values.reshape(groups, 2 * size, nent * rows)
+    matrix = gridding.reshape(nent * rows, slab_rows)
+    vmem = pl.BlockSpec(memory_space=pltpu.VMEM)
+    dma = pltpu.SemaphoreType.DMA
+    f32 = jnp.float32
+    return pl.pallas_call(
+        functools.partial(grid_kernel, ngrid, ndp, size),
+        out_shape=(jax.ShapeDtypeStruct((share, slab_rows), f32),
+                   jax.ShapeDtypeStruct(weights.shape[1:], f32)),
+        in_specs=[vmem] * 4,
+        out_specs=(vmem, vmem),
+        scratch_shapes=[
+            pltpu.VMEM((groups, ndp, share, slab_rows), f32),
+            pltpu.VMEM((groups, ndp, share, slab_rows), f32),
+            pltpu.VMEM((groups, ndp, share, slab_rows), f32),
+            pltpu.VMEM((groups, ndp - 1, share, slab_rows), f32),
+            pltpu.VMEM((groups, share, slab_rows), f32),
+            pltpu.VMEM((groups - 1, share, slab_rows), f32),
+            pltpu.VMEM((ndp - 1,) + weights.shape[1:], f32),
+            dma((groups,)), dma((groups,)), dma((groups, ndp - 1)), dma((groups, ndp - 1)),
+            dma((groups - 1,)), dma((groups - 1,)), dma((ndp - 1,)), dma((ndp - 1,)),
+        ],
+        compiler_params=pltpu.CompilerParams(
+            collective_id=1, has_side_effects=True, vmem_limit_bytes=52 * 2 ** 20),
+    )(values, matrix, jnp.asarray(first_table(size, ndp)), weights)
+
+
+def mirrored(weights, ndp):
+    size = weights.shape[0]
     turned = jnp.transpose(weights, (2, 1, 0))
-    kept = each * ndp
-    front = turned[:kept]
-    back = jnp.roll(jnp.flip(turned, (0, 2)), (1, 1), (0, 2))[:kept]
-    both = jnp.stack([front, back])
-    both = both.reshape(2, ndp, each, both.shape[2], size).transpose(1, 0, 2, 3, 4)
-    both = lax.psum_scatter(both, "dp", scatter_dimension=0, tiled=True)[0]
+    flipped = jnp.roll(jnp.flip(turned, (0, 2)), (1, 1), (0, 2))
+    each, half = size // 2 // ndp, size // 2
+    shares = [
+        jnp.concatenate([field[d * each:(d + 1) * each], field[half:half + 1]])
+        for d in range(ndp) for field in (turned, flipped)
+    ]
+    return jnp.stack(shares).reshape(ndp, -1, size)
+
+
+def spectral_weight(both, ngrid):
     front, back = both[0], both[1]
     edge = lax.ppermute(back[:, :1], "grid", [(g, (ngrid - g) % ngrid) for g in range(ngrid)])
     rest = lax.ppermute(back[:, 1:], "grid", [(g, ngrid - 1 - g) for g in range(ngrid)])
@@ -161,42 +318,30 @@
     return 0.5 * (front + back)
 
 
-def gridded(intensities, gridding, dest_slab, ngrid, ndp, each):
-    nent, rows, size = intensities.shape
-    slab_rows = gridding.shape[2]
-    planes = slab_rows // size
-    member = dest_slab == jnp.arange(ngrid, dtype=jnp.int32)[None, :]
-    values = jnp.where(member[:, None, :, None], intensities[:, :, None, :], 0)
-    values = values.reshape(nent * rows, ngrid * size)
-    matrix = gridding.reshape(nent * rows, slab_rows)
-    product = lax.dot_general(
-        values, matrix, (((0,), (0,)), ((), ())), preferred_element_type=jnp.float32
-    ).reshape(ngrid, size, slab_rows)
-    table = first_table(size, ndp).reshape(ndp * 2 * each, size)
-    spread = jnp.stack([
-        lax.dot_general(jnp.asarray(table), product[s], (((1,), (0,)), ((), ())), precision=HIGH)
-        for s in range(ngrid)
-    ], axis=1).reshape(ndp, 2 * each, ngrid, slab_rows)
-    part = lax.psum_scatter(spread, "dp", scatter_dimension=0, tiled=True)[0]
-    part = jnp.transpose(part, (1, 0, 2))
-    part = lax.psum_scatter(part, "grid", scatter_dimension=0, tiled=True)[0]
-    return part.reshape(2, each, planes, size)
+def unpacked(part, planes, size, ndp):
+    part = part.reshape(2, -1, planes, size)
+    lead = lax.axis_index("dp") == 0
+    real, imag, zero = part[0], part[1], jnp.zeros_like(part[1, :1])
+    real = jnp.concatenate([real, jnp.where(lead, imag[:1], zero)])
+    imag = jnp.concatenate([jnp.where(lead, zero, imag[:1]), imag[1:], zero])
+    return jnp.stack([real, imag])
 
 
 def body(intensities, gridding, dest_slab, spectral_weights):
     ngrid = lax.axis_size("grid")
     ndp = lax.axis_size("dp")
-    nent, rows, size = intensities.shape
-    each = half_size(size, ndp)
-    weight = spectral_weight(spectral_weights[0], ngrid, ndp, each, size)
-    part = gridded(intensities, gridding, dest_slab, ngrid, ndp, each)
+    size = intensities.shape[2]
+    planes = gridding.shape[2] // size
+    part, both = gridded(
+        intensities, gridding, dest_slab, mirrored(spectral_weights[0], ndp), ngrid, ndp)
+    weight = spectral_weight(both.reshape(2, -1, spectral_weights.shape[2], size), ngrid)
+    part = unpacked(part, planes, size, ndp)
     ahead, back = complex_table(size, -1.0), complex_table(size, 1.0)
     rows_done = along("ckxy,cydj->dkxj", part, ahead)
     columns = lax.all_to_all(rows_done, "grid", split_axis=3, concat_axis=2, tiled=True)
     spectrum = along("ckxj,cxdm->dkjm", columns, ahead)
-    share = lax.dynamic_slice_in_dim(
-        jnp.asarray(counts(size, each * ndp), jnp.float32), lax.axis_index("dp") * each, each
-    )
+    share = lax.dynamic_index_in_dim(
+        jnp.asarray(counts(size, ndp)), lax.axis_index("dp"), keepdims=False)
     power = share[:, None, None] * (spectrum[0] * spectrum[0] + spectrum[1] * spectrum[1])
     rho, sigma = multipliers(power.reshape(-1, size), weight.reshape(-1, size))
     fields = jnp.stack([sigma, rho]).reshape((2, 1) + power.shape) * spectrum[None]

time: 474 us -> 284 us (0.60)
  waiting for transfers between devices: 241 us -> 41.9 us
  Pallas kernels: 60.8 us -> 130 us
  local copies, waits for them, and re-layouts: 80.2 us -> 50 us
  matrix products: 38.5 us -> 11 us
    unnamed x7 -> x1, waiting for transfers between devices: 202 us -> 0.02 us
    pallas_call x0 -> x1, Pallas kernels: none -> 69.3 us  [gridded(): pl.pallas_call(functools.partial(grid_kernel, ngrid, ndp, size), out_shap...]
    dot_general x9 -> x0, matrix products: 27.5 us -> none  [the longest x8 15.4 us: gridded(): lax.dot_general(jnp.asarray(table), product[s], (((1,), (0,)), ((), ())),...]
    another operation x10 -> x0, local copies, waits for them, and re-layouts: 25.2 us -> none  [gridded(): jnp.stack([lax.dot_general(jnp.asarray(table), product[s], (((1,), (0,)),...]
    unnamed x41 -> x23, local copies, waits for them, and re-layouts: 26.8 us -> 21.7 us
  transfers between devices with their start and end apart: 7 -> 4, of which waited for: 5 -> 3; matrix products, arithmetic and copies ran while one was open for 3% -> 1% of each run, Pallas kernels for 0% -> 0%
where the time goes in v2:
time: 284 us; the launch traced here: 283 us
  Pallas kernels  130 us (46%)
  local copies, waits for them, and re-layouts  50 us (18%)
  waiting for transfers between devices  41.9 us (15%)
  blocking collectives  18.8 us (7%)
  between operations  14.4 us (5%)
  matrix products  11 us (4%)
  other arithmetic  9.21 us (3%)
  starting transfers between devices  7.81 us (3%)
    pallas_call x1, Pallas kernels, gridded(): pl.pallas_call(functools.partial(grid_kernel, ngrid, ndp, size), out_shap...  69.3 us
    pallas_call x1, Pallas kernels, multipliers(): pl.pallas_call(functools.partial(scalar_kernel, ngrid, ndp), out_shape=(s...  60.6 us
    all_gather x1, waiting for transfers between devices, body(): whole = lax.all_gather(planes, 'dp', axis=0, tiled=False)  34.3 us
    unnamed x23, local copies, waits for them, and re-layouts  21.7 us
    all_to_all x1, blocking collectives, body(): lax.all_to_all(columns, 'grid', split_axis=3, concat_axis=4, tiled=True)  18.8 us
    dot_general x6, matrix products, along(): return jnp.einsum(form, field, table, precision=HIGH)  11 us
    all_to_all x2, local copies, waits for them, and re-layouts, body(): lax.all_to_all(columns, 'grid', split_axis=3, concat_axis=4, tiled=True)  10.8 us
    transpose x3, local copies, waits for them, and re-layouts, along(): return jnp.einsum(form, field, table, precision=HIGH)  7.21 us
  transfers between devices with their start and end apart: 4, of which 3 were waited for; matrix products, arithmetic and copies ran while one was open for 1% of the time, Pallas kernels for 0%

profile of v2, /device:TPU:0, one launch (start us, length us, event | category | flops | bytes accessed | tf_op | source)
XLA Modules:
  0.0 283.1 jit_solution(4935469180655539489)
XLA Ops:
  7.2 1.9 copy.56
  9.1 0.0 copy-start.4
  9.1 0.1 slice.132
  9.2 0.5 copy-done.5
  9.7 0.1 broadcast_in_dim.40
  9.8 0.1 eq.24
  9.9 0.3 copy-done.4
  10.1 1.0 copy.55
  11.2 0.1 slice.106
  11.2 1.2 slice.108
  12.5 0.3 slice_maximum_fusion
  12.8 0.1 fusion.33
  13.0 0.1 fusion.30
  13.1 0.1 fusion.27
  13.3 0.1 pad_add_fusion
  13.4 0.1 broadcast_add_fusion
  13.4 0.1 broadcast_compare_fusion
  13.5 0.6 copy-done.1
  14.2 0.1 broadcast_in_dim.43
  14.3 0.0 copy-start
  14.3 2.3 bitcast_select_fusion.values_ref
  16.6 69.3 %shard_map.143 = (f32[32,2048]{1,0:T(8,128)S(1)}, f32[544,128]{1,0:T(8,128)S(1)}) custom-call(bf16[4,256,2048]{2,1,0:T(8,128)(2,1)} %bitcast_select_fusion.values_ref, bf16[2048,2048]{1,0:T(8,128)(2,1)} %bitcast.164, f32[128,128]{1,0:T(8,128)S(1)} %copy-done, f32[4,544,128]{2,1,0:T(8,128)S(1)} %bitcast.160), custom_call_target="tpu_custom_call" | custom-call | tf_op jit(solution)/shard_map/pallas_call | solution.py:279
  85.9 0.0 copy-start.2
  86.1 0.1 pad.8.clone
  86.1 0.1 maximum_bitcast_fusion.3
  86.2 0.6 copy-done.2
  86.9 0.4 convolution_bitcast_fusion.3
  87.3 1.9 copy.57
  89.1 2.5 reshape.128
  91.7 3.4 %all-to-all-start = ((f32[8,1,8704]{2,1,0:T(1,128)}), f32[8,1,8704]{2,1,0:T(1,128)S(1)}, u32[]{:S(2)}, u32[]{:S(2)}) async-start(f32[8,1,8704]{2,1,0:T(1,128)} %reshape.128), calls=%async_computation | async-start | bytes 557056 | tf_op jit(solution)/shard_map/all_to_all | solution.py:341
  95.1 0.0 all-gather.3.cloned.1.call-start
  95.2 3.5 %collective-permute-start.1 = (f32[17,15,128]{2,1,0:T(8,128)S(1)}, f32[17,15,128]{2,1,0:T(8,128)S(1)}, u32[]{:S(2)}, u32[]{:S(2)}) collective-permute-start(f32[17,15,128]{2,1,0:T(8,128)S(1)} %slice.140), channel_id=1, source_target_pairs={{0,7},{1,6},{2,5},{3,4},{4,3},{5,2},{6,1},{7,0},{8,15},{9,14},{10,... | collective-permute-start | bytes 391688 | tf_op jit(solution)/shard_map/ppermute | solution.py:316
  98.7 0.8 collective-permute-start
  99.6 0.7 dynamic-slice_bitcast_fusion
  100.3 0.1 mul.48
  100.3 0.1 mul.49
  100.4 6.7 %collective-permute-done.1 = f32[17,15,128]{2,1,0:T(8,128)S(1)} collective-permute-done((f32[17,15,128]{2,1,0:T(8,128)S(1)}, f32[17,15,128]{2,1,0:T(8,128)S(1)}, u32[]{:S(2)}, u32[]{:S(2)}) %collective-permute-start.1) | collective-permute-done | bytes 130592 | tf_op jit(solution)/shard_map/ppermute | solution.py:316
  107.2 0.7 fusion.36.weight_ref
  107.9 0.8 all-to-all-done
  108.8 0.6 broadcast.103
  109.4 1.3 reduce
  110.7 3.6 %reshape.129 = f32[128,2,16,17]{3,2,1,0:T(8,128)} reshape(f32[8,8704]{1,0:T(8,128)S(1)} %reduce) | data formatting | bytes 557056
  114.3 3.6 %copy.82 = f32[2,17,8,16,16]{3,2,4,0,1:T(8,128)S(1)} copy(f32[2,17,8,16,16]{1,3,0,4,2:T(8,128)} %bitcast.165) | data formatting | bytes 557056 | tf_op jit(solution)/shard_map/all_to_all | solution.py:341
  117.9 0.6 reshape.113
  118.5 0.0 copy-start.3
  118.5 0.4 convolution_bitcast_fusion.2
  118.9 0.8 bitcast_multiply_fusion.power_ref
  119.7 60.6 %shard_map.144 = (f32[272,128]{1,0:T(8,128)}, f32[272,128]{1,0:T(8,128)}) custom-call(f32[272,128]{1,0:T(8,128)} %bitcast_multiply_fusion.power_ref, f32[272,128]{1,0:T(8,128)} %fusion.36.weight_ref), custom_call_target="tpu_custom_call" | custom-call | tf_op jit(solution)/shard_map/pallas_call | solution.py:134
  180.4 1.0 maximum_bitcast_fusion.2
  181.4 0.6 convolution_bitcast_fusion.1
  182.0 4.5 %copy.61 = f32[2,2,17,128,16]{2,4,1,0,3:T(8,128)} copy(f32[2,2,17,128,16]{3,4,1,2,0:T(8,128)S(1)} %convolution_bitcast_fusion.1) | data formatting | bytes 1114112 | tf_op jit(solution)/shard_map/fckjm,cmdx->fdkxj/transpose | solution.py:57
  186.5 4.9 %reshape.130 = f32[8,1,17408]{2,1,0:T(1,128)S(1)} reshape(f32[128,2,2,16,17]{4,3,2,1,0:T(8,128)} %bitcast.161) | data formatting | bytes 1114112
  191.4 18.8 %all_to_all.36 = f32[8,1,17408]{2,1,0:T(1,128)S(1)} all-to-all(f32[8,1,17408]{2,1,0:T(1,128)S(1)} %reshape.130), channel_id=1, replica_groups=mesh['dp'=4,'grid'=8] {'grid'}, dimensions={0} | all-to-all | bytes 1114112 | tf_op jit(solution)/shard_map/all_to_all | solution.py:349
  210.2 2.0 reduce.1
  212.2 6.7 %reshape.131 = f32[128,2,2,16,17]{4,3,2,1,0:T(8,128)} reshape(f32[8,17408]{1,0:T(8,128)S(1)} %reduce.1) | data formatting | bytes 1114112
  218.9 7.2 %copy.85 = f32[2,2,17,16,8,16]{5,4,3,1,2,0:T(8,128)} copy(f32[2,2,17,16,8,16]{2,5,1,0,3,4:T(8,128)} %bitcast.162) | data formatting | bytes 1114112 | tf_op jit(solution)/shard_map/all_to_all | solution.py:349
  226.1 3.6 %reshape.118 = f32[2,2,17,16,128,1]{4,3,1,2,0,5:T(8,128)S(1)} reshape(f32[2,2,17,16,8,16]{5,4,3,1,2,0:T(8,128)} %copy.85) | data formatting | bytes 1114112 | tf_op jit(solution)/shard_map/all_to_all | solution.py:349
  229.7 0.6 convolution_bitcast_fusion
  230.3 0.8 copy.65
  231.2 0.0 all-gather.3.cloned.1.call-update
  231.2 34.3 %all-gather.3.cloned.1.call-done = f32[8,2,17,16,128]{4,3,2,1,0:T(8,128)} async-done(((f32[2,2,17,16,128]{4,3,2,1,0:T(8,128)}), f32[8,2,17,16,128]{4,3,2,1,0:T(8,128)}) %all-gather.3.cloned.1.call-update) | async-done | bytes 2228240 | tf_op jit(solution)/shard_map/all_gather | solution.py:351
  265.5 1.8 fusion.38
  267.3 4.5 %fusion.3 = f32[16,128,128]{2,1,0:T(8,128)} fusion(f32[4,2,17,128,1]{3,2,0,4,1:T(8,128)S(1)} %copy-done.6, f32[4,1,2,17,16,128]{5,4,3,2,1,0:T(8,128)S(1)} %get-tuple-element.13), kind=kOutput, calls=%fused_computation.6 | convolution fusion | flops 427819008 | bytes 2232320 | tf_op jit(solution)/shard_map/dckxy,dckz->xyz/dot_general | solution.py:57
  271.8 4.5 %fusion.2 = f32[16,128,128]{2,1,0:T(8,128)} fusion(f32[4,2,17,128,1]{3,2,0,4,1:T(8,128)S(1)} %copy-done.6, f32[4,1,2,17,16,128]{5,4,3,2,1,0:T(8,128)S(1)} %get-tuple-element.14), kind=kOutput, calls=%fused_computation.5 | convolution fusion | flops 427819008 | bytes 2232320 | tf_op jit(solution)/shard_map/dckxy,dckz->xyz/dot_general | solution.py:57
  (27 shorter events, 0.3 us)
Async XLA Ops:
  9.1 0.7 copy-start.5
  9.1 1.0 copy-start.4
  13.1 1.0 copy-start.1
  14.3 2.3 copy-start
  85.9 1.0 copy-start.2
  91.7 17.1 %all-to-all-start = ((f32[8,1,8704]{2,1,0:T(1,128)}), f32[8,1,8704]{2,1,0:T(1,128)S(1)}, u32[]{:S(2)}, u32[]{:S(2)}) async-start(f32[8,1,8704]{2,1,0:T(1,128)} %reshape.128), calls=%async_computation | async-start | bytes 557056 | tf_op jit(solution)/shard_map/all_to_all | solution.py:341
  95.1 170.4 %all-gather.3.cloned.1.call-start = ((), (), s32[]{:S(2)}) async-start(), calls=%async_computation.2 | async-start | bytes 2785280 | tf_op jit(solution)/shard_map/all_gather | solution.py:351
  95.2 12.0 %collective-permute-start.1 = (f32[17,15,128]{2,1,0:T(8,128)S(1)}, f32[17,15,128]{2,1,0:T(8,128)S(1)}, u32[]{:S(2)}, u32[]{:S(2)}) collective-permute-start(f32[17,15,128]{2,1,0:T(8,128)S(1)} %slice.140), channel_id=1, source_target_pairs={{0,7},{1,6},{2,5},{3,4},{4,3},{5,2},{6,1},{7,0},{8,15},{9,14},{10,... | collective-permute-start | bytes 391688 | tf_op jit(solution)/shard_map/ppermute | solution.py:316
  98.7 8.5 %collective-permute-start = (f32[17,1,128]{2,1,0:T(1,128)S(1)}, f32[17,1,128]{2,1,0:T(1,128)S(1)}, u32[]{:S(2)}, u32[]{:S(2)}) collective-permute-start(f32[17,1,128]{2,1,0:T(1,128)S(1)} %slice.139), channel_id=1, source_target_pairs={{0,0},{1,7},{2,6},{3,5},{4,4},{5,3},{6,2},{7,1},{8,8},{9,15},{10,1... | collective-permute-start | bytes 26120 | tf_op jit(solution)/shard_map/ppermute | solution.py:315
  118.5 62.9 %copy-start.3 = (f32[2,128,2,128,1,1]{3,1,0,2,5,4:T(8,128)S(1)}, f32[2,128,2,128,1,1]{3,1,0,2,5,4:T(8,128)}, u32[]{:S(2)}) copy-start(f32[2,128,2,128,1,1]{3,1,0,2,5,4:T(8,128)} %constant.56) | copy-start | bytes 786436
  265.5 1.8 copy-start.6
Sparse Core Ops, SparseCore 0:
  231.3 34.1 all-gather.2
